TPU v7x, 32 devices: a whole 2x2x4 slice. The times are simulated.
32 devices in a mesh: group: 2 (over y), section: 2 (over core), expert: 8 (over z, x).
Axes of the slice: x: 2, y: 2, z: 4, core: 2. Of those that a mesh axis runs over, the one named last changes fastest.
Arguments:
- activations: bfloat16 [64, 6144], P(('group', 'expert')), parts along dimension 0, may hold values from -6 to 6
- routes: int32 [2, 64, 2], P('section', ('group', 'expert')), parts along dimension 1, may hold values from 0 to 7, as said below
- norm_gain: bfloat16 [2, 6144], P('section'), may hold values from 0.099609375 to 1.8984375
- router: bfloat16 [2, 6144, 8], P('section'), may hold values from -0.078125 to 0.078125
- w_gate: bfloat16 [2, 6144, 1024], P('section', None, 'expert'), may hold values from -0.078125 to 0.078125
- w_up: bfloat16 [2, 6144, 1024], P('section', None, 'expert'), may hold values from -0.078125 to 0.078125
- w_down: bfloat16 [2, 1024, 6144], P('section', 'expert'), may hold values from -0.1875 to 0.1875
Outputs:
- section_out: bfloat16 [2, 64, 6144], P('section', ('group', 'expert')), parts along dimension 1
There are 2 independent parts, one for each index of `group`. A program takes and returns all parts, laid end to end along the dimension named above; an argument that names none is the same for every part. Nothing has to cross between parts.
Inputs may be any that keep to these rules, and one draw needn't show every extreme that they name: `routes`: each row names 2 different experts; within the rows of one device (aligned blocks of 4 rows) no expert is named by more than 2 rows, and in each layer expert 0 is named by exactly 2 rows of some device.
All inputs are finite; a program needn't handle non-finite values.
Results may differ from a plain program's by a relative error of at most 0.005.
Values may be sent and summed in bfloat16 or wider, within the bound.
A program may use at most 64 MiB of HBM per device.

v0:
```python
import jax
import jax.numpy as jnp
from jax import lax
from jax.sharding import PartitionSpec as P

EXPERTS = 8
EF = 1
CAP = 2


EPSILON = 1e-05


def shifted(block, axis, distance):
    devices = range(lax.axis_size(axis))
    route = [(i - distance, i) for i in devices if i - distance in devices]
    return lax.ppermute(block, axis, route)


def expert_compute(slot_rows, gate_w, up_w, down_w):
    source_count, item_count, model_width = slot_rows.shape
    flattened = slot_rows.reshape(source_count * item_count, model_width)
    gate_pre = jnp.dot(flattened, gate_w, preferred_element_type=jnp.float32)
    up_pre = jnp.dot(flattened, up_w, preferred_element_type=jnp.float32)
    hidden = (jax.nn.silu(gate_pre) * up_pre).astype(jnp.bfloat16)
    partial_out = jnp.dot(hidden, down_w, preferred_element_type=jnp.float32).astype(jnp.bfloat16)
    return partial_out.reshape(source_count, item_count, model_width)


def moe_layer(inputs, route_ids, gain_row, router_w, gate_w, up_w, down_w):
    row_count, model_width = inputs.shape
    shards = lax.axis_size("expert") // EF
    widened = inputs.astype(jnp.float32)
    inv_rms = lax.rsqrt(jnp.mean(widened * widened, axis=-1, keepdims=True) + EPSILON)
    normed = (widened * inv_rms * gain_row.astype(jnp.float32)).astype(jnp.bfloat16)
    logits = jnp.dot(normed, router_w, preferred_element_type=jnp.float32)
    expert_ids = lax.broadcasted_iota(jnp.int32, (1, 1, EXPERTS), 2)
    picked = route_ids[:, :, None] == expert_ids
    chosen = jnp.sum(jnp.where(picked, logits[:, None, :], 0.0), axis=-1)
    gate_probs = jax.nn.softmax(chosen, axis=-1)
    held_ids = lax.broadcasted_iota(jnp.int32, (1, 1, EF), 2)
    member = (route_ids[:, :, None] == held_ids).astype(jnp.float32)
    weight = jnp.sum(member * gate_probs[:, :, None], axis=1)
    marks = jnp.sum(member, axis=1).astype(jnp.int32)
    rank = jnp.cumsum(marks, axis=0, dtype=jnp.int32) - marks
    slot_iota = lax.broadcasted_iota(jnp.int32, (1, 1, CAP), 2)
    place = ((rank[:, :, None] == slot_iota) & (marks[:, :, None] == 1)).astype(jnp.float32)
    buffer = jnp.einsum(
        "rkc,rd->kcd", place.astype(jnp.bfloat16), normed, preferred_element_type=jnp.float32
    ).astype(jnp.bfloat16)
    outgoing = jnp.repeat(buffer, shards, axis=0)
    shaped = expert_compute(
        lax.all_to_all(outgoing, "expert", split_axis=0, concat_axis=0, tiled=True),
        gate_w,
        up_w,
        down_w,
    )
    returned = lax.all_to_all(shaped, "expert", split_axis=0, concat_axis=0, tiled=True)
    summed = jnp.sum(returned.reshape(EF, shards, CAP, model_width), axis=1, dtype=jnp.float32)
    combine_w = place * weight[:, :, None]
    expert_sum = jnp.einsum("rkc,kcd->rd", combine_w, summed)
    return (widened + expert_sum).astype(jnp.bfloat16)


def hand_on(produced):
    return shifted(produced, "section", 1)


def per_device(activations, routes, norm_gain, router, w_gate, w_up, w_down):
    section_count = lax.axis_size("section")
    section_idx = lax.axis_index("section")
    section_routes = routes[0]
    gain_row = norm_gain[0]
    router_w = router[0]
    gate_w = w_gate[0]
    up_w = w_up[0]
    down_w = w_down[0]
    current = activations
    result = jnp.zeros_like(activations)
    for phase_idx in range(section_count):
        produced = moe_layer(current, section_routes, gain_row, router_w, gate_w, up_w, down_w)
        result = jnp.where(section_idx == phase_idx, produced, result)
        if phase_idx + 1 < section_count:
            current = hand_on(produced)
    return result[None]


def solution(mesh):
    in_specs = (
        P(("group", "expert"), None),
        P("section", ("group", "expert"), None),
        P("section", None),
        P("section", None, None),
        P("section", None, "expert"),
        P("section", None, "expert"),
        P("section", "expert", None),
    )
    out_specs = P("section", ("group", "expert"), None)
    return jax.shard_map(
        per_device, mesh=mesh, in_specs=in_specs, out_specs=out_specs, check_vma=False
    )
```

profile of v0, /device:TPU:0, one launch (start us, length us, event | category | flops | bytes accessed | tf_op | source)
XLA Modules:
  0.0 69.6 jit_solution(15190092848470300071)
XLA Ops:
  0.0 0.9 %mul.97 = f32[1,6144]{1,0:T(1,128)S(1)} convert(bf16[1,6144]{1,0:T(2,128)(2,1)} %param.9) | non-fusion elementwise | flops 6144 | bytes 36864 | tf_op jit(solution)/shard_map/mul | solution.py:35
  0.9 1.0 %fusion.30 = f32[4]{0:T(128)S(1)} fusion(bf16[4,6144]{1,0:T(4,128)(2,1)} %param.7), kind=kLoop, calls=%fused_computation.30 | loop fusion | flops 73724 | bytes 49168 | tf_op jit(solution)/shard_map/reduce_sum | solution.py:34
  1.9 0.7 broadcast_compare_fusion
  2.6 1.3 %fusion.38 = f32[4,8]{1,0:T(4,128)S(1)} fusion(bf16[1,6144,8]{1,2,0:T(8,128)(2,1)} %param.10, bf16[4,6144]{1,0:T(4,128)(2,1)} %param.7, f32[6144]{0:T(1024)S(1)} %bitcast.52, f32[4]{0:T(128)S(1)} %add_rsqrt_fusion.1), kind=kOutput, calls=%fused_computation.38 | convolution fusion | flops 491520 | bytes 172176 | tf_op jit(solution)/shard_map/dot_general | solution.py:36
  3.8 0.8 %select_reduce_fusion.1 = f32[4,2]{0,1:T(2,128)S(1)} fusion(f32[4,8]{1,0:T(4,128)S(1)} %fusion.38, s32[4,2]{0,1:T(2,128)} %bitcast.58), kind=kLoop, calls=%fused_computation.53 | loop fusion | flops 184 | bytes 192 | tf_op jit(solution)/shard_map/reduce_sum | solution.py:39
  4.9 0.2 fusion.54
  5.2 0.2 reduce-window.7
  5.4 1.0 %convolution_convert_fusion.3 = bf16[2,6144]{1,0:T(2,128)(2,1)S(1)} fusion(pred[4,2]{1,0:T(4,128)(4,1)S(1)} %fusion.56, bf16[4,6144]{1,0:T(4,128)(2,1)} %param.7, f32[6144]{0:T(1024)S(1)} %bitcast.53, f32[4]{0:T(128)S(1)} %add_rsqrt_fusion.1), kind=kOutput, calls=%fused_computation.9 | convolution fusion | flops 208912 | bytes 98328 | tf_op jit(solution)/shard_map/rkc,rd->kcd/dot_general | solution.py:48
  6.6 15.0 %all_to_all.20 = bf16[8,2,6144]{2,1,0:T(2,128)(2,1)S(1)} all-to-all(bf16[8,2,6144]{2,1,0:T(2,128)(2,1)S(1)} %reshape.376), channel_id=1, replica_groups=mesh['group'=2,'section'=2,'expert'=8] {'expert'}, dimensions={0} | all-to-all | bytes 393216 | tf_op jit(solution)/shard_map/all_to_all | solution.py:53
  21.7 1.7 %fusion.12 = f32[16,128]{1,0:T(8,128)S(1)} fusion(bf16[16,6144]{1,0:T(8,128)(2,1)S(1)} %reshape.377, bf16[1,6144,128]{2,1,0:T(8,128)(2,1)} %param.11), kind=kOutput, calls=%fused_computation.18 | convolution fusion | flops 25165824 | bytes 1777664 | tf_op jit(solution)/shard_map/dot_general | solution.py:23
  23.4 0.6 convolution_convert_fusion.1
  24.1 0.2 reshape.378
  24.2 10.7 %all_to_all.21 = bf16[8,2,6144]{2,1,0:T(2,128)(2,1)S(1)} all-to-all(bf16[8,2,6144]{2,1,0:T(2,128)(2,1)S(1)} %reshape.378), channel_id=1, replica_groups=mesh['group'=2,'section'=2,'expert'=8] {'expert'}, dimensions={0} | all-to-all | bytes 393216 | tf_op jit(solution)/shard_map/all_to_all | solution.py:58
  35.0 0.2 convert_reduce_fusion.1
  35.1 1.0 %fusion = bf16[4,6144]{1,0:T(4,128)(2,1)S(1)} fusion(bf16[2,6144]{1,0:T(2,128)(2,1)S(1)} %convert_reduce_fusion.1, bf16[4,6144]{1,0:T(4,128)(2,1)} %param.7, pred[4,2]{1,0:T(4,128)(4,1)} %copy-done.6, bf16[4]{0:T(256)(128)(2,1)S(1)} %get-tuple-element.5), kind=kOutput, calls=%fused_computation.4 | convolution fusion | flops 172040 | bytes 122896 | tf_op jit(solution)/shard_map/rkc,kcd->rd/dot_general | solution.py:61
  36.2 1.3 %collective-permute-start = (bf16[4,6144]{1,0:T(4,128)(2,1)S(1)}, bf16[4,6144]{1,0:T(4,128)(2,1)S(1)}, u32[]{:S(2)}, u32[]{:S(2)}) collective-permute-start(bf16[4,6144]{1,0:T(4,128)(2,1)S(1)} %fusion), channel_id=1, source_target_pairs={{0,8},{1,9},{2,10},{3,11},{4,12},{5,13},{6,14},{7,15},{16,24},{17,... | collective-permute-start | bytes 147464 | tf_op jit(solution)/shard_map/ppermute | solution.py:17
  37.5 0.9 %collective-permute-done = bf16[4,6144]{1,0:T(4,128)(2,1)S(1)} collective-permute-done((bf16[4,6144]{1,0:T(4,128)(2,1)S(1)}, bf16[4,6144]{1,0:T(4,128)(2,1)S(1)}, u32[]{:S(2)}, u32[]{:S(2)}) %collective-permute-start) | collective-permute-done | bytes 49184 | tf_op jit(solution)/shard_map/ppermute | solution.py:17
  38.3 0.2 fusion.33
  38.5 0.4 copy-done.2
  39.0 0.5 copy-done.7
  39.4 1.0 %convolution_convert_fusion.2 = bf16[2,6144]{1,0:T(2,128)(2,1)S(1)} fusion(pred[4,2]{1,0:T(4,128)(4,1)} %copy-done.6, bf16[4,6144]{1,0:T(4,128)(2,1)S(1)} %collective-permute-done, f32[4]{0:T(128)S(1)} %add_rsqrt_fusion, f32[6144]{0:T(1024)} %bitcast.54), kind=kOutput, calls=%fused_computation.8 | convolution fusion | flops 208912 | bytes 98328 | tf_op jit(solution)/shard_map/rkc,rd->kcd/dot_general | solution.py:48
  40.4 0.8 %reshape.379 = bf16[8,2,6144]{2,1,0:T(2,128)(2,1)} broadcast(bf16[2,6144]{1,0:T(2,128)(2,1)S(1)} %convolution_convert_fusion.2), dimensions={1,2} | broadcast | bytes 221184 | tf_op jit(solution)/shard_map/reshape | solution.py:51
  41.2 3.4 %all-to-all-start.2 = ((bf16[8,2,6144]{2,1,0:T(2,128)(2,1)}), bf16[8,2,6144]{2,1,0:T(2,128)(2,1)S(1)}, u32[]{:S(2)}, u32[]{:S(2)}) async-start(bf16[8,2,6144]{2,1,0:T(2,128)(2,1)} %reshape.379), calls=%async_computation.2 | async-start | bytes 393216 | tf_op jit(solution)/shard_map/all_to_all | solution.py:53
  44.6 8.7 %all-to-all-done.2 = bf16[8,2,6144]{2,1,0:T(2,128)(2,1)S(1)} async-done(((bf16[8,2,6144]{2,1,0:T(2,128)(2,1)}), bf16[8,2,6144]{2,1,0:T(2,128)(2,1)S(1)}, u32[]{:S(2)}, u32[]{:S(2)}) %all-to-all-start.2) | async-done | bytes 196640 | tf_op jit(solution)/shard_map/all_to_all | solution.py:53
  53.4 1.7 %fusion.10 = f32[16,128]{1,0:T(8,128)S(1)} fusion(bf16[16,6144]{1,0:T(8,128)(2,1)S(1)} %reshape.380, bf16[1,6144,128]{2,1,0:T(8,128)(2,1)} %param.11), kind=kOutput, calls=%fused_computation.16 | convolution fusion | flops 25165824 | bytes 1777664 | tf_op jit(solution)/shard_map/dot_general | solution.py:23
  55.1 0.6 convolution_convert_fusion
  55.7 0.8 %reshape.381 = bf16[8,2,6144]{2,1,0:T(2,128)(2,1)} reshape(bf16[16,6144]{1,0:T(8,128)(2,1)S(1)} %convolution_convert_fusion) | data formatting | bytes 393216 | tf_op jit(solution)/shard_map/reshape | solution.py:27
  56.6 3.4 %all-to-all-start.3 = ((bf16[8,2,6144]{2,1,0:T(2,128)(2,1)}), bf16[8,2,6144]{2,1,0:T(2,128)(2,1)S(1)}, u32[]{:S(2)}, u32[]{:S(2)}) async-start(bf16[8,2,6144]{2,1,0:T(2,128)(2,1)} %reshape.381), calls=%async_computation.3 | async-start | bytes 393216 | tf_op jit(solution)/shard_map/all_to_all | solution.py:58
  60.0 1.2 %fusion.36 = f32[4,8]{1,0:T(4,128)S(1)} fusion(bf16[1,6144,8]{1,2,0:T(8,128)(2,1)} %param.10, bf16[4,6144]{1,0:T(4,128)(2,1)} %copy-done.2, f32[4]{0:T(128)} %copy-done.7, f32[6144]{0:T(1024)} %bitcast.55), kind=kOutput, calls=%fused_computation.36 | convolution fusion | flops 491520 | bytes 172176 | tf_op jit(solution)/shard_map/dot_general | solution.py:36
  61.4 0.2 fusion.55
  61.6 6.2 %all-to-all-done.3 = bf16[8,2,6144]{2,1,0:T(2,128)(2,1)S(1)} async-done(((bf16[8,2,6144]{2,1,0:T(2,128)(2,1)}), bf16[8,2,6144]{2,1,0:T(2,128)(2,1)S(1)}, u32[]{:S(2)}, u32[]{:S(2)}) %all-to-all-start.3) | async-done | bytes 196640 | tf_op jit(solution)/shard_map/all_to_all | solution.py:58
  68.0 1.7 %fusion.3 = bf16[1,4,6144]{2,1,0:T(4,128)(2,1)} fusion(bf16[2,6144]{1,0:T(2,128)(2,1)S(1)} %convert_reduce_fusion, bf16[4,6144]{1,0:T(4,128)(2,1)} %copy-done.2, bf16[4,6144]{1,0:T(4,128)(2,1)} %copy-done.5, pred[]{:T(512)S(6)} %eq.106, pred[]{:T(512)S(6)} %eq.95, pred[4,2]{1,0:T(4,128)(4,1)} %copy-done.6, bf16[4]{0:T(256)(128)(2,1)S(1)} %fusion.55), kind=kOutput, calls=%fused_computation.7 | convolution fusion | flops 221192 | bytes 172050 | tf_op jit(solution)/shard_map/rkc,kcd->rd/dot_general | solution.py:61
  (32 shorter events, 1.1 us)
Async XLA Ops:
  0.0 23.4 %copy-start = (bf16[1,128,6144]{2,1,0:T(8,128)(2,1)S(1)}, bf16[1,128,6144]{2,1,0:T(8,128)(2,1)}, u32[]{:S(2)}) copy-start(bf16[1,128,6144]{2,1,0:T(8,128)(2,1)} %param.13) | copy-start | bytes 4718596
  0.9 5.7 %copy-start.3 = (f32[1,6144]{1,0:T(1,128)}, f32[1,6144]{1,0:T(1,128)S(1)}, u32[]{:S(2)}) copy-start(f32[1,6144]{1,0:T(1,128)S(1)} %mul.97) | copy-start | bytes 73732
  2.6 20.9 %copy-start.1 = (bf16[1,6144,128]{2,1,0:T(8,128)(2,1)S(1)}, bf16[1,6144,128]{2,1,0:T(8,128)(2,1)}, u32[]{:S(2)}) copy-start(bf16[1,6144,128]{2,1,0:T(8,128)(2,1)} %param.12) | copy-start | bytes 4718596
  5.4 1.2 %copy-start.6 = (pred[4,2]{1,0:T(4,128)(4,1)}, pred[4,2]{1,0:T(4,128)(4,1)S(1)}, u32[]{:S(2)}) copy-start(pred[4,2]{1,0:T(4,128)(4,1)S(1)} %fusion.56) | copy-start | bytes 28
  36.2 1.3 %copy-start.5 = (bf16[4,6144]{1,0:T(4,128)(2,1)}, bf16[4,6144]{1,0:T(4,128)(2,1)S(1)}, u32[]{:S(2)}) copy-start(bf16[4,6144]{1,0:T(4,128)(2,1)S(1)} %fusion) | copy-start | bytes 147460
  36.2 2.2 %collective-permute-start = (bf16[4,6144]{1,0:T(4,128)(2,1)S(1)}, bf16[4,6144]{1,0:T(4,128)(2,1)S(1)}, u32[]{:S(2)}, u32[]{:S(2)}) collective-permute-start(bf16[4,6144]{1,0:T(4,128)(2,1)S(1)} %fusion), channel_id=1, source_target_pairs={{0,8},{1,9},{2,10},{3,11},{4,12},{5,13},{6,14},{7,15},{16,24},{17,... | collective-permute-start | bytes 147464 | tf_op jit(solution)/shard_map/ppermute | solution.py:17
  38.3 0.6 copy-start.2
  39.0 0.5 copy-start.7
  41.2 12.1 %all-to-all-start.2 = ((bf16[8,2,6144]{2,1,0:T(2,128)(2,1)}), bf16[8,2,6144]{2,1,0:T(2,128)(2,1)S(1)}, u32[]{:S(2)}, u32[]{:S(2)}) async-start(bf16[8,2,6144]{2,1,0:T(2,128)(2,1)} %reshape.379), calls=%async_computation.2 | async-start | bytes 393216 | tf_op jit(solution)/shard_map/all_to_all | solution.py:53
  55.1 6.0 %copy-start.4 = (s32[1,4,2]{1,2,0:T(2,128)S(1)}, s32[1,4,2]{1,2,0:T(2,128)}, u32[]{:S(2)}) copy-start(s32[1,4,2]{1,2,0:T(2,128)} %param.8) | copy-start | bytes 100
  56.6 11.2 %all-to-all-start.3 = ((bf16[8,2,6144]{2,1,0:T(2,128)(2,1)}), bf16[8,2,6144]{2,1,0:T(2,128)(2,1)S(1)}, u32[]{:S(2)}, u32[]{:S(2)}) async-start(bf16[8,2,6144]{2,1,0:T(2,128)(2,1)} %reshape.381), calls=%async_computation.3 | async-start | bytes 393216 | tf_op jit(solution)/shard_map/all_to_all | solution.py:58
where the time goes:
time: 70.5 us; the launch traced here: 69.6 us
  blocking collectives  25.7 us (36%)
  waiting for transfers between devices  15.7 us (22%)
  matrix products  11.8 us (17%)
  starting transfers between devices  8.07 us (11%)
  other arithmetic  4.84 us (7%)
  local copies, waits for them, and re-layouts  3.28 us (5%)
    all_to_all x1, blocking collectives, moe_layer(): lax.all_to_all(outgoing, 'expert', split_axis=0, concat_axis=0, tiled=True)  15 us
    all_to_all x1, blocking collectives, moe_layer(): lax.all_to_all(shaped, 'expert', split_axis=0, concat_axis=0, tiled=True)  10.7 us
    all_to_all x1, waiting for transfers between devices, moe_layer(): lax.all_to_all(outgoing, 'expert', split_axis=0, concat_axis=0, tiled=True)  8.68 us
    all_to_all x1, waiting for transfers between devices, moe_layer(): lax.all_to_all(shaped, 'expert', split_axis=0, concat_axis=0, tiled=True)  6.17 us
    dot_general x2, matrix products, expert_compute(): gate_pre = jnp.dot(flattened, gate_w, preferred_element_type=jnp.float32)  3.44 us
    all_to_all x1, starting transfers between devices, moe_layer(): lax.all_to_all(outgoing, 'expert', split_axis=0, concat_axis=0, tiled=True)  3.39 us
    all_to_all x1, starting transfers between devices, moe_layer(): lax.all_to_all(shaped, 'expert', split_axis=0, concat_axis=0, tiled=True)  3.39 us
    dot_general x2, matrix products, moe_layer(): expert_sum = jnp.einsum('rkc,kcd->rd', combine_w, summed)  2.7 us
  transfers between devices with their start and end apart: 3, of which 3 were waited for; matrix products, arithmetic and copies ran while one was open for 2% of the time, Pallas kernels for 0%

commit v1 on v0

v1 whole, which is shorter than its diff:
```python
import functools

import jax
import jax.numpy as jnp
from jax import lax
from jax.experimental import pallas as pl
from jax.experimental.pallas import tpu as pltpu
from jax.sharding import PartitionSpec as P

EPSILON = 1e-05
CAP = 2
CHUNKS = 4


def far_first(n):
    return sorted(range(1, n), key=lambda k: (abs(k - n // 2), k))


def for_peers(n, me, body):
    if n <= 8:
        for k in far_first(n):
            body(lax.rem(me + k, n))
    else:
        def step(k, carry):
            body(lax.rem(me + k, n))
            return carry
        lax.fori_loop(1, n, step, 0)


def column(row):
    r = row.shape[1]
    eye = lax.broadcasted_iota(jnp.int32, (r, r), 0) == lax.broadcasted_iota(jnp.int32, (r, r), 1)
    return jnp.sum(jnp.where(eye, jnp.broadcast_to(row, (r, r)), 0.0), axis=1, keepdims=True)


def kernel(
    n, chunks,
    x_h, routes_ref, gain_h, router_h, wg_h, wu_h, wd_h,
    o_ref,
    x_v, gain_v, router_v, wgu_v, wd_v, normed_v, slot, gbuf, sbuf, rbuf, cw_v, cw_in, x1_v,
    lsem, wsem, gs_sem, gr_sem, ps_sem, pr_sem, msem,
):
    group = lax.axis_index("group")
    section = lax.axis_index("section")
    me = lax.axis_index("expert")
    rows, width = x_h.shape
    dk = width // chunks
    hid = wd_h.shape[1]

    small = [
        pltpu.make_async_copy(x_h, x_v, lsem.at[0]),
        pltpu.make_async_copy(gain_h, gain_v, lsem.at[1]),
        pltpu.make_async_copy(router_h, router_v, lsem.at[2]),
    ]
    for copy in small:
        copy.start()

    barrier = pltpu.get_barrier_semaphore()

    def greet(sec, peer):
        pl.semaphore_signal(
            barrier, inc=1, device_id=(group, sec, peer), device_id_type=pl.DeviceIdType.MESH
        )

    greet(1 - section, me)
    for_peers(n, me, lambda peer: greet(section, peer))

    @pl.when(section == 1)
    def _():
        for_peers(n, me, lambda peer: greet(0, peer))

    weights = []
    for c in range(chunks):
        part = pl.ds(c * dk, dk)
        weights.append([
            pltpu.make_async_copy(wg_h.at[0, part, :], wgu_v.at[part, pl.ds(0, hid)], wsem.at[0, c]),
            pltpu.make_async_copy(wu_h.at[0, part, :], wgu_v.at[part, pl.ds(hid, hid)], wsem.at[1, c]),
        ])
    down_copy = pltpu.make_async_copy(wd_h.at[0], wd_v, wsem.at[2, 0])
    for pair in weights:
        for copy in pair:
            copy.start()
    down_copy.start()

    def remote(src, dst, send_sem, recv_sem, sec, peer):
        return pltpu.make_async_remote_copy(
            src_ref=src, dst_ref=dst, send_sem=send_sem, recv_sem=recv_sem,
            device_id=(group, sec, peer), device_id_type=pl.DeviceIdType.MESH,
        )

    def wait_bytes(ref, sem):
        pltpu.make_async_copy(ref, ref, sem).wait()

    small[0].wait()
    small[1].wait()

    @pl.when(section == 0)
    def _():
        pl.semaphore_wait(barrier, 2 * n - 1)

    @pl.when(section == 1)
    def _():
        pl.semaphore_wait(barrier, n)

    first = column(routes_ref[0:1, :].astype(jnp.float32))
    second = column(routes_ref[1:2, :].astype(jnp.float32))
    marks = jnp.where((first == 0.0) | (second == 0.0), 1.0, 0.0)
    row_iota = lax.broadcasted_iota(jnp.int32, (rows, 1), 0)
    rank = jnp.zeros((rows, 1), jnp.float32)
    for q in range(rows - 1):
        rank += jnp.where(row_iota > q, jnp.broadcast_to(marks[q:q + 1, :], (rows, 1)), 0.0)
    places = [jnp.where(rank == float(c), marks, 0.0) for c in range(CAP)]

    def send_rows(src_ref):
        wide = src_ref[...].astype(jnp.float32)
        inv_rms = lax.rsqrt(jnp.mean(wide * wide, axis=-1, keepdims=True) + EPSILON)
        for c in range(chunks):
            part = pl.ds(c * dk, dk)
            normed = src_ref[:, part].astype(jnp.float32) * inv_rms * gain_v[:, part].astype(jnp.float32)
            normed = normed.astype(jnp.bfloat16)
            normed_v[:, part] = normed
            normed = normed.astype(jnp.float32)
            picked = [jnp.sum(normed * place, axis=0, keepdims=True) for place in places]
            block = jnp.concatenate(picked, axis=0).astype(jnp.bfloat16)
            slot[c] = block
            gbuf[c, me] = block
            for_peers(n, me, lambda peer: remote(
                slot.at[c], gbuf.at[c, me], gs_sem.at[c], gr_sem.at[c], section, peer).start())

    def combine_weights():
        logits = lax.dot_general(
            normed_v[...], router_v[...], (((1,), (1,)), ((), ())),
            preferred_element_type=jnp.float32,
        )
        ids = lax.broadcasted_iota(jnp.int32, logits.shape, 1).astype(jnp.float32)
        one = jnp.sum(jnp.where(ids == first, logits, 0.0), axis=1, keepdims=True)
        two = jnp.sum(jnp.where(ids == second, logits, 0.0), axis=1, keepdims=True)
        top = jnp.maximum(one, two)
        e_one, e_two = jnp.exp(one - top), jnp.exp(two - top)
        total = e_one + e_two
        weight = jnp.where(first == 0.0, e_one / total, 0.0) + jnp.where(second == 0.0, e_two / total, 0.0)
        lane = lax.broadcasted_iota(jnp.int32, (rows, 128), 1)
        packed = jnp.where(lane == 0, places[0] * weight, jnp.where(lane == 1, places[1] * weight, 0.0))
        cw_v[...] = packed

    def expert(layer, own):
        acc = jnp.zeros((CAP * n, 2 * hid), jnp.float32)
        for c in range(chunks):
            for copy in weights[c]:
                copy.wait()
            wait_bytes(gbuf.at[c, pl.ds(0, n - 1)], gr_sem.at[c])
            lhs = gbuf[c].astype(jnp.float32).reshape(CAP * n, dk).astype(jnp.bfloat16)
            acc += jnp.dot(lhs, wgu_v[pl.ds(c * dk, dk), :], preferred_element_type=jnp.float32)
        gate, up = acc[:, :hid], acc[:, hid:]
        hidden = (gate / (1.0 + jnp.exp(-gate)) * up).astype(jnp.bfloat16)
        down_copy.wait()
        for c in range(chunks):
            part = jnp.dot(hidden, wd_v[:, pl.ds(c * dk, dk)], preferred_element_type=jnp.float32)
            sbuf[c] = part.reshape(n, CAP, dk).astype(jnp.bfloat16)

            def send(peer):
                remote(
                    sbuf.at[c, peer], rbuf.at[c, me], ps_sem.at[c], pr_sem.at[c], 1, peer
                ).start()

            for_peers(n, me, send)
            if own:
                rbuf[c, me] = sbuf[c, me]
            else:
                send(me)

    def combine(c, count, base, cw):
        wait_bytes(rbuf.at[c, pl.ds(0, count)], pr_sem.at[c])
        summed = jnp.sum(rbuf[c].astype(jnp.float32), axis=0)
        total = base + cw[:, 0:1] * summed[0:1, :] + cw[:, 1:2] * summed[1:2, :]
        return total.astype(jnp.bfloat16)

    def drain_rows():
        for c in range(chunks):
            wait_bytes(gbuf.at[c, pl.ds(0, n - 1)], gs_sem.at[c])

    def drain_partials(count):
        for c in range(chunks):
            wait_bytes(sbuf.at[c, pl.ds(0, count)], ps_sem.at[c])

    @pl.when(section == 0)
    def _():
        send_rows(x_v)
        small[2].wait()
        combine_weights()
        weigh = remote(cw_v, cw_in, msem.at[0], msem.at[1], 1, me)
        weigh.start()
        expert(0, False)
        drain_rows()
        weigh.wait_send()
        drain_partials(n)
        wait_bytes(o_ref.at[0], msem.at[3])

    @pl.when(section == 1)
    def _():
        wait_bytes(cw_in, msem.at[1])
        cw0 = cw_in[...]
        for c in range(chunks):
            part = pl.ds(c * dk, dk)
            x1_v[:, part] = combine(c, n, x_v[:, part].astype(jnp.float32), cw0)
        send_rows(x1_v)
        back = remote(x1_v, o_ref.at[0], msem.at[2], msem.at[3], 0, me)
        back.start()
        small[2].wait()
        combine_weights()
        expert(1, True)
        cw1 = cw_v[...]
        for c in range(chunks):
            part = pl.ds(c * dk, dk)
            o_ref[0, :, part] = combine(c, n - 1, x1_v[:, part].astype(jnp.float32), cw1)
        drain_rows()
        back.wait_send()
        drain_partials(n - 1)


def per_device(activations, routes, norm_gain, router, w_gate, w_up, w_down):
    rows, width = activations.shape
    n = lax.axis_size("expert")
    hid = w_down.shape[1]
    chunks = CHUNKS
    dk = width // chunks
    bf16, f32 = jnp.bfloat16, jnp.float32
    dma = pltpu.SemaphoreType.DMA
    anywhere = pl.BlockSpec(memory_space=pl.ANY)
    vmem = pl.BlockSpec(memory_space=pltpu.VMEM)
    return pl.pallas_call(
        functools.partial(kernel, n, chunks),
        out_shape=jax.ShapeDtypeStruct((1, rows, width), bf16),
        in_specs=[anywhere, vmem, anywhere, anywhere, anywhere, anywhere, anywhere],
        out_specs=vmem,
        scratch_shapes=[
            pltpu.VMEM((rows, width), bf16),
            pltpu.VMEM((1, width), bf16),
            pltpu.VMEM((router.shape[2], width), bf16),
            pltpu.VMEM((width, 2 * hid), bf16),
            pltpu.VMEM((hid, width), bf16),
            pltpu.VMEM((rows, width), bf16),
            pltpu.VMEM((chunks, CAP, dk), bf16),
            pltpu.VMEM((chunks, n, CAP, dk), bf16),
            pltpu.VMEM((chunks, n, CAP, dk), bf16),
            pltpu.VMEM((chunks, n, CAP, dk), bf16),
            pltpu.VMEM((rows, 128), f32),
            pltpu.VMEM((rows, 128), f32),
            pltpu.VMEM((rows, width), bf16),
            dma((3,)),
            dma((3, chunks)),
            dma((chunks,)),
            dma((chunks,)),
            dma((chunks,)),
            dma((chunks,)),
            dma((4,)),
        ],
        compiler_params=pltpu.CompilerParams(
            collective_id=0, has_side_effects=True, vmem_limit_bytes=48 * 2**20
        ),
    )(activations, routes[0].T, norm_gain, router[0].T, w_gate, w_up, w_down)


def solution(mesh):
    in_specs = (
        P(("group", "expert"), None),
        P("section", ("group", "expert"), None),
        P("section", None),
        P("section", None, None),
        P("section", None, "expert"),
        P("section", None, "expert"),
        P("section", "expert", None),
    )
    out_specs = P("section", ("group", "expert"), None)
    return jax.shard_map(
        per_device, mesh=mesh, in_specs=in_specs, out_specs=out_specs, check_vma=False
    )
```

time: 70.5 us -> 36.1 us (0.51)
  the two profiles are of different devices: /device:TPU:0 before, /device:TPU:1 now
where the time goes in v1:
time: 36.1 us; the launch traced here: 35.8 us
  Pallas kernels  27.8 us (77%)
  local copies, waits for them, and re-layouts  7.95 us (22%)
    pallas_call x1, Pallas kernels, per_device(): pl.pallas_call(functools.partial(kernel, n, chunks), out_shape=jax.ShapeD...  27.8 us
    unnamed x15, local copies, waits for them, and re-layouts  7.95 us

profile of v1, /device:TPU:1, one launch (start us, length us, event | category | flops | bytes accessed | tf_op | source)
XLA Modules:
  0.0 35.8 jit_solution(16042667323621048141)
XLA Ops:
  0.0 0.0 copy-start
  0.0 1.4 %copy-done = bf16[1,6144,128]{2,1,0:T(8,128)(2,1)S(1)} copy-done((bf16[1,6144,128]{2,1,0:T(8,128)(2,1)S(1)}, bf16[1,6144,128]{2,1,0:T(8,128)(2,1)}, u32[]{:S(2)}) %copy-start) | copy-done | bytes 1572888
  1.4 0.0 copy-start.1
  1.4 1.4 %copy-done.1 = bf16[1,6144,128]{2,1,0:T(8,128)(2,1)S(1)} copy-done((bf16[1,6144,128]{2,1,0:T(8,128)(2,1)S(1)}, bf16[1,6144,128]{2,1,0:T(8,128)(2,1)}, u32[]{:S(2)}) %copy-start.1) | copy-done | bytes 1572888
  2.8 0.0 copy-start.2
  2.8 1.4 %copy-done.2 = bf16[1,128,6144]{2,1,0:T(8,128)(2,1)S(1)} copy-done((bf16[1,128,6144]{2,1,0:T(8,128)(2,1)S(1)}, bf16[1,128,6144]{2,1,0:T(8,128)(2,1)}, u32[]{:S(2)}) %copy-start.2) | copy-done | bytes 1572888
  4.2 0.0 copy-start.3
  4.2 0.9 %copy-done.3 = bf16[1,6144,8]{1,2,0:T(8,128)(2,1)S(1)} copy-done((bf16[1,6144,8]{1,2,0:T(8,128)(2,1)S(1)}, bf16[1,6144,8]{1,2,0:T(8,128)(2,1)}, u32[]{:S(2)}) %copy-start.3) | copy-done | bytes 98328
  5.1 0.0 copy-start.4
  5.1 0.8 %copy-done.4 = bf16[4,6144]{1,0:T(4,128)(2,1)S(1)} copy-done((bf16[4,6144]{1,0:T(4,128)(2,1)S(1)}, bf16[4,6144]{1,0:T(4,128)(2,1)}, u32[]{:S(2)}) %copy-start.4) | copy-done | bytes 49176
  5.9 0.0 copy-start.5
  5.9 0.7 %copy-done.5 = bf16[1,6144]{1,0:T(2,128)(2,1)S(1)} copy-done((bf16[1,6144]{1,0:T(2,128)(2,1)S(1)}, bf16[1,6144]{1,0:T(2,128)(2,1)}, u32[]{:S(2)}) %copy-start.5) | copy-done | bytes 12312
  6.7 0.0 copy-start.6
  6.7 0.7 %copy-done.6 = s32[1,4,2]{1,2,0:T(2,128)S(1)} copy-done((s32[1,4,2]{1,2,0:T(2,128)S(1)}, s32[1,4,2]{1,2,0:T(2,128)}, u32[]{:S(2)}) %copy-start.6) | copy-done | bytes 56
  7.3 27.8 %shard_map.73 = bf16[1,4,6144]{2,1,0:T(4,128)(2,1)S(1)} custom-call(bf16[4,6144]{1,0:T(4,128)(2,1)S(1)} %copy-done.4, s32[2,4]{1,0:T(2,128)S(1)} %bitcast.7, bf16[1,6144]{1,0:T(2,128)(2,1)S(1)} %copy-done.5, bf16[8,6144]{1,0:T(8,128)(2,1)S(1)} %bitcast.6, bf16[1,6144,128]{2,1,0:T(8,128)(2,1)S(1)} %copy-done, bf16[1,6144,128]{2,1,0:T(8,128)(2,1)S(1)} %copy-done.1, ...), custom_call_target="tpu_custom_call" | custom-call | tf_op jit(solution)/shard_map/pallas_call | solution.py:231
  35.1 0.6 %copy.9 = bf16[1,4,6144]{2,1,0:T(4,128)(2,1)} copy(bf16[1,4,6144]{2,1,0:T(4,128)(2,1)S(1)} %shard_map.73) | data formatting | bytes 98304
Async XLA Ops:
  0.0 1.4 %copy-start = (bf16[1,6144,128]{2,1,0:T(8,128)(2,1)S(1)}, bf16[1,6144,128]{2,1,0:T(8,128)(2,1)}, u32[]{:S(2)}) copy-start(bf16[1,6144,128]{2,1,0:T(8,128)(2,1)} %wg_h.1) | copy-start | bytes 4718596
  1.4 1.4 %copy-start.1 = (bf16[1,6144,128]{2,1,0:T(8,128)(2,1)S(1)}, bf16[1,6144,128]{2,1,0:T(8,128)(2,1)}, u32[]{:S(2)}) copy-start(bf16[1,6144,128]{2,1,0:T(8,128)(2,1)} %wu_h.1) | copy-start | bytes 4718596
  2.8 1.4 %copy-start.2 = (bf16[1,128,6144]{2,1,0:T(8,128)(2,1)S(1)}, bf16[1,128,6144]{2,1,0:T(8,128)(2,1)}, u32[]{:S(2)}) copy-start(bf16[1,128,6144]{2,1,0:T(8,128)(2,1)} %wd_h.1) | copy-start | bytes 4718596
  4.2 0.9 %copy-start.3 = (bf16[1,6144,8]{1,2,0:T(8,128)(2,1)S(1)}, bf16[1,6144,8]{1,2,0:T(8,128)(2,1)}, u32[]{:S(2)}) copy-start(bf16[1,6144,8]{1,2,0:T(8,128)(2,1)} %param.10) | copy-start | bytes 294916
  5.1 0.8 %copy-start.4 = (bf16[4,6144]{1,0:T(4,128)(2,1)S(1)}, bf16[4,6144]{1,0:T(4,128)(2,1)}, u32[]{:S(2)}) copy-start(bf16[4,6144]{1,0:T(4,128)(2,1)} %x_h.1) | copy-start | bytes 147460
  5.9 0.7 %copy-start.5 = (bf16[1,6144]{1,0:T(2,128)(2,1)S(1)}, bf16[1,6144]{1,0:T(2,128)(2,1)}, u32[]{:S(2)}) copy-start(bf16[1,6144]{1,0:T(2,128)(2,1)} %gain_h.1) | copy-start | bytes 36868
  6.7 0.7 %copy-start.6 = (s32[1,4,2]{1,2,0:T(2,128)S(1)}, s32[1,4,2]{1,2,0:T(2,128)}, u32[]{:S(2)}) copy-start(s32[1,4,2]{1,2,0:T(2,128)} %param.8) | copy-start | bytes 100

commit v2 on v1

--- a/solution.py
+++ b/solution.py
@@ -35,9 +35,9 @@
 
 def kernel(
     n, chunks,
-    x_h, routes_ref, gain_h, router_h, wg_h, wu_h, wd_h,
+    x_h, routes_h, gain_h, router_h, wg_h, wu_h, wd_h,
     o_ref,
-    x_v, gain_v, router_v, wgu_v, wd_v, normed_v, slot, gbuf, sbuf, rbuf, cw_v, cw_in, x1_v,
+    x_v, routes_ref, gain_v, router_v, wgu_v, wd_v, normed_v, slot, gbuf, sbuf, rbuf, cw_v, cw_in, x1_v,
     lsem, wsem, gs_sem, gr_sem, ps_sem, pr_sem, msem,
 ):
     group = lax.axis_index("group")
@@ -51,6 +51,7 @@
         pltpu.make_async_copy(x_h, x_v, lsem.at[0]),
         pltpu.make_async_copy(gain_h, gain_v, lsem.at[1]),
         pltpu.make_async_copy(router_h, router_v, lsem.at[2]),
+        pltpu.make_async_copy(routes_h, routes_ref, lsem.at[3]),
     ]
     for copy in small:
         copy.start()
@@ -102,6 +103,7 @@
     def _():
         pl.semaphore_wait(barrier, n)
 
+    small[3].wait()
     first = column(routes_ref[0:1, :].astype(jnp.float32))
     second = column(routes_ref[1:2, :].astype(jnp.float32))
     marks = jnp.where((first == 0.0) | (second == 0.0), 1.0, 0.0)
@@ -226,15 +228,16 @@
     dk = width // chunks
     bf16, f32 = jnp.bfloat16, jnp.float32
     dma = pltpu.SemaphoreType.DMA
-    anywhere = pl.BlockSpec(memory_space=pl.ANY)
+    hbm = pl.BlockSpec(memory_space=pltpu.HBM)
     vmem = pl.BlockSpec(memory_space=pltpu.VMEM)
     return pl.pallas_call(
         functools.partial(kernel, n, chunks),
-        out_shape=jax.ShapeDtypeStruct((1, rows, width), bf16),
-        in_specs=[anywhere, vmem, anywhere, anywhere, anywhere, anywhere, anywhere],
+        out_shape=pltpu.VMEM((1, rows, width), bf16),
+        in_specs=[hbm] * 7,
         out_specs=vmem,
         scratch_shapes=[
             pltpu.VMEM((rows, width), bf16),
+            pltpu.VMEM((routes.shape[2], rows), jnp.int32),
             pltpu.VMEM((1, width), bf16),
             pltpu.VMEM((router.shape[2], width), bf16),
             pltpu.VMEM((width, 2 * hid), bf16),
@@ -247,7 +250,7 @@
             pltpu.VMEM((rows, 128), f32),
             pltpu.VMEM((rows, 128), f32),
             pltpu.VMEM((rows, width), bf16),
-            dma((3,)),
+            dma((4,)),
             dma((3, chunks)),
             dma((chunks,)),
             dma((chunks,)),
@@ -258,7 +261,7 @@
         compiler_params=pltpu.CompilerParams(
             collective_id=0, has_side_effects=True, vmem_limit_bytes=48 * 2**20
         ),
-    )(activations, routes[0].T, norm_gain, router[0].T, w_gate, w_up, w_down)
+    )(*[pltpu.with_memory_space_constraint(v, pltpu.HBM) for v in (activations, routes[0].T, norm_gain, router[0].T, w_gate, w_up, w_down)])
 
 
 def solution(mesh):

time: 36.1 us -> 28.3 us (0.78)
  local copies, waits for them, and re-layouts: 7.95 us -> 0.62 us
    unnamed x15 -> x1, local copies, waits for them, and re-layouts: 7.95 us -> 0.62 us
where the time goes in v2:
time: 28.3 us; the launch traced here: 28.2 us
  Pallas kernels  27.6 us (98%)
  local copies, waits for them, and re-layouts  0.62 us (2%)
    pallas_call x1, Pallas kernels, per_device(): pl.pallas_call(functools.partial(kernel, n, chunks), out_shape=pltpu.VMEM...  27.6 us
    unnamed x1, local copies, waits for them, and re-layouts  0.62 us

profile of v2, /device:TPU:1, one launch (start us, length us, event | category | flops | bytes accessed | tf_op | source)
XLA Modules:
  0.0 28.2 jit_solution(15451535499308302134)
XLA Ops:
  0.0 27.6 %shard_map.73 = bf16[1,4,6144]{2,1,0:T(4,128)(2,1)S(1)} custom-call(bf16[4,6144]{1,0:T(4,128)(2,1)} %x_h.1, s32[2,4]{1,0:T(2,128)} %bitcast.7, bf16[1,6144]{1,0:T(2,128)(2,1)} %gain_h.1, bf16[8,6144]{1,0:T(8,128)(2,1)} %bitcast.6, bf16[1,6144,128]{2,1,0:T(8,128)(2,1)} %wg_h.1, bf16[1,6144,128]{2,1,0:T(8,128)(2,1)} %wu_h.1, bf16[1,128,6144]{2,1,0:T(8,128)(2,1)} %wd_h.1), custom_call_target="tpu_custom_call" | custom-call | tf_op jit(solution)/shard_map/pallas_call | solution.py:233
  27.6 0.6 %copy.9 = bf16[1,4,6144]{2,1,0:T(4,128)(2,1)} copy(bf16[1,4,6144]{2,1,0:T(4,128)(2,1)S(1)} %shard_map.73) | data formatting | bytes 98304

commit v3 on v2

--- a/solution.py
+++ b/solution.py
@@ -12,14 +12,19 @@
 CHUNKS = 4
 
 
-def far_first(n):
-    return sorted(range(1, n), key=lambda k: (abs(k - n // 2), k))
+def partner(me, k):
+    peer, bit = me, 1
+    while bit <= k:
+        if k & bit:
+            peer = peer + bit * (1 - 2 * lax.rem(me // bit, 2))
+        bit *= 2
+    return peer
 
 
 def for_peers(n, me, body):
-    if n <= 8:
-        for k in far_first(n):
-            body(lax.rem(me + k, n))
+    if n in (2, 4, 8):
+        for k in range(n - 1, 0, -1):
+            body(partner(me, k))
     else:
         def step(k, carry):
             body(lax.rem(me + k, n))

time: 28.3 us -> 27 us (0.954)
  Pallas kernels: 27.6 us -> 26.2 us
    pallas_call x1, Pallas kernels: 27.6 us -> 26.2 us  [per_device(): pl.pallas_call(functools.partial(kernel, n, chunks), out_shape=pltpu.VMEM...]
where the time goes in v3:
time: 27 us; the launch traced here: 26.9 us
  Pallas kernels  26.2 us (97%)
  local copies, waits for them, and re-layouts  0.62 us (2%)
    pallas_call x1, Pallas kernels, per_device(): pl.pallas_call(functools.partial(kernel, n, chunks), out_shape=pltpu.VMEM...  26.2 us
    unnamed x1, local copies, waits for them, and re-layouts  0.62 us

profile of v3, /device:TPU:1, one launch (start us, length us, event | category | flops | bytes accessed | tf_op | source)
XLA Modules:
  0.0 26.9 jit_solution(13028136344307107368)
XLA Ops:
  0.0 26.2 %shard_map.73 = bf16[1,4,6144]{2,1,0:T(4,128)(2,1)S(1)} custom-call(bf16[4,6144]{1,0:T(4,128)(2,1)} %x_h.1, s32[2,4]{1,0:T(2,128)} %bitcast.7, bf16[1,6144]{1,0:T(2,128)(2,1)} %gain_h.1, bf16[8,6144]{1,0:T(8,128)(2,1)} %bitcast.6, bf16[1,6144,128]{2,1,0:T(8,128)(2,1)} %wg_h.1, bf16[1,6144,128]{2,1,0:T(8,128)(2,1)} %wu_h.1, bf16[1,128,6144]{2,1,0:T(8,128)(2,1)} %wd_h.1), custom_call_target="tpu_custom_call" | custom-call | tf_op jit(solution)/shard_map/pallas_call | solution.py:238
  26.2 0.6 %copy.9 = bf16[1,4,6144]{2,1,0:T(4,128)(2,1)} copy(bf16[1,4,6144]{2,1,0:T(4,128)(2,1)S(1)} %shard_map.73) | data formatting | bytes 98304
